TPU v7x, 32 devices: a whole 2x2x4 slice. The times are simulated.
32 devices in a mesh: poles: 2 (over y), row: 4 (over z), col: 4 (over x, core).
Axes of the slice: x: 2, y: 2, z: 4, core: 2. Of those that a mesh axis runs over, the one named last changes fastest.
Arguments:
- root_inverse: float32 [16, 1024, 8, 1024], P('poles', 'row', None, 'col'), parts along dimension 0, may hold values from -6 to 6
- factor_panel: float32 [16, 1024, 2048], P('poles', 'col', 'row'), parts along dimension 0, may hold values from -0.0625 to 0.0625
- struct_mask: int32 [2, 32], replicated, may hold values 0 or 1
- child_diag_inverse: float32 [1024, 4096], P('row', ('poles', 'col')), parts along dimension 1, may hold values from -6 to 6
Outputs:
- panel_inverse: float32 [4096, 8, 1024], P(('poles', 'col'), None, 'row'), parts along dimension 0
- child_inverse: float32 [1024, 4096], P('row', ('poles', 'col')), parts along dimension 1
There are 2 independent parts, one for each index of `poles`. A program takes and returns all parts, laid end to end along the dimension named above; an argument that names none is the same for every part. Nothing has to cross between parts.
All inputs are finite; a program needn't handle non-finite values.
Results may differ from a plain program's by a relative error of at most 0.0001.
Values sent between devices are 32-bit elements; how exact they have to be, the bound alone decides.
A program may use at most 192 MiB of HBM per device.

v0:
```python
import jax
import jax.numpy as jnp
from jax import lax
from jax.sharding import PartitionSpec as P

precise = lax.Precision.HIGHEST


def broadcast(block, axis, holder):
    block = jnp.where(lax.axis_index(axis) == holder, block, jnp.zeros_like(block))
    return lax.psum(block, axis)


def local(root_inverse, factor_panel, struct_mask, child_diag_inverse):
    row_count = lax.axis_size("row")
    col_count = lax.axis_size("col")
    row_index = lax.axis_index("row")
    col_index = lax.axis_index("col")
    local_rows = root_inverse.shape[0]
    block_width = root_inverse.shape[1]
    local_cols = root_inverse.shape[2]
    rows_here = local_rows * block_width
    cols_here = local_cols * block_width
    matrix = root_inverse.reshape(rows_here, cols_here)
    mask_float = struct_mask.astype(jnp.float32)
    children = mask_float.shape[0]
    mask_cols = lax.dynamic_index_in_dim(
        mask_float.reshape(children, local_cols, col_count), col_index, 2, False
    )
    mask_rows = lax.dynamic_index_in_dim(
        mask_float.reshape(children, local_rows, row_count), row_index, 2, False
    )
    panel = lax.all_gather(factor_panel, "row", axis=2, tiled=True)
    total = panel.shape[2]
    child_width = total // children
    slice_width = total // col_count
    spread_cols = jnp.repeat(mask_cols.T, child_width, axis=1)
    masked_panel = (panel * spread_cols[:, None, :]).reshape(cols_here, total)
    summed = lax.psum_scatter(
        -jnp.dot(matrix, masked_panel, precision=precise).T, "col", scatter_dimension=0, tiled=True
    )
    start_col = col_index * slice_width
    row_spread = jnp.repeat(mask_rows.T, child_width, axis=1)
    row_mask_here = lax.dynamic_slice_in_dim(row_spread, start_col, slice_width, 1)
    upper = summed.reshape(slice_width, local_rows, block_width) * row_mask_here.T[:, :, None]
    ratio = row_count // col_count
    own_rows = lax.dynamic_index_in_dim(
        panel.reshape(local_rows, ratio, block_width, total), row_index // col_count, 1, False
    )
    child_here = start_col // child_width
    holder = row_index % col_count
    partner_rows = broadcast(own_rows, "col", holder)
    left_rows = lax.dynamic_slice_in_dim(partner_rows, child_here * child_width, child_width, 2)
    left_mask = lax.dynamic_index_in_dim(mask_rows, child_here, 0, False)
    left_rows = (left_rows * left_mask[:, None, None]).reshape(rows_here, child_width)
    partial_block = jnp.einsum(
        "iu,vi->uv", left_rows, upper.reshape(slice_width, rows_here), precision=precise
    )
    reduced = lax.psum_scatter(partial_block, "row", scatter_dimension=0, tiled=True)
    return (upper, child_diag_inverse - reduced)


def solution(mesh):
    return jax.shard_map(
        local,
        mesh=mesh,
        in_specs=(
            P("poles", "row", None, "col"),
            P("poles", "col", "row"),
            P(),
            P("row", ("poles", "col")),
        ),
        out_specs=(P(("poles", "col"), None, "row"), P("row", ("poles", "col"))),
        check_vma=False,
    )
```

profile of v0, /device:TPU:0, one launch (start us, length us, event | category | flops | bytes accessed | tf_op | source)
XLA Modules:
  0.0 1032.1 jit_solution(1916085299608278126)
XLA Ops:
  7.2 0.0 all-gather.2.cloned.1.call-start
  7.2 0.7 all-gather.2.cloned.1.call-update
  7.9 0.0 reduce-scatter.3.cloned.1.call-start
  8.0 0.7 convert_element_type.3
  8.6 0.1 reshape.31
  8.7 15.9 %copy.11 = f32[256,8,8,256]{3,1,2,0:T(8,128)} copy(f32[256,8,8,256]{3,2,1,0:T(8,128)} %bitcast.18) | data formatting | bytes 33554432
  24.6 0.2 dynamic-slice_reduce_fusion
  24.8 274.3 %all-gather.2.cloned.1.call-done = f32[8,256,2048]{2,1,0:T(8,128)} async-done(((f32[8,256,512]{2,1,0:T(8,128)}), f32[8,256,2048]{2,1,0:T(8,128)}) %all-gather.2.cloned.1.call-update) | async-done | bytes 16777232 | tf_op jit(solution)/shard_map/all_gather | solution.py:33
  299.1 0.1 broadcast_in_dim.11
  299.1 17.2 %broadcast_select_fusion = (f32[8,256,2048]{2,1,0:T(8,128)}, f32[8,256,2048]{2,1,0:T(8,128)}) fusion(f32[8,256,2048]{2,1,0:T(8,128)} %all-gather.2.cloned.1.call-done, pred[]{:T(512)S(6)} %eq.5, f32[8,2048]{1,0:T(8,128)S(1)} %bitcast.22), kind=kLoop, calls=%fused_computation.4 | loop fusion | flops 8388608 | bytes 50397184 | tf_op jit(solution)/shard_map/jit(_where)/select_n | solution.py:10
  316.4 215.9 %convolution_negate_fusion = f32[2048,2048]{1,0:T(8,128)} fusion(f32[2048,2048]{1,0:T(8,128)} %bitcast.17, f32[2048,2048]{1,0:T(8,128)} %bitcast.19), kind=kOutput, calls=%fused_computation | convolution fusion | flops 103083409408 | bytes 50331648 | tf_op jit(solution)/shard_map/dot_general | solution.py:40
  532.3 0.0 reduce-scatter.3.cloned.1.call-update
  532.3 0.0 all-reduce.2.cloned.1.call-start
  532.4 0.7 all-reduce.2.cloned.1.call-update
  533.0 0.0 reduce-scatter.5.cloned.1.call-start
  533.1 0.2 dynamic-slice_reduce_fusion.2
  533.3 0.1 broadcast_in_dim.12
  533.4 123.3 %reduce-scatter.3.cloned.1.call-done = f32[512,2048]{1,0:T(8,128)} async-done(((f32[2048,2048]{1,0:T(8,128)}), f32[512,2048]{1,0:T(8,128)}) %reduce-scatter.3.cloned.1.call-update) | async-done | bytes 4194320 | tf_op jit(solution)/shard_map/reduce_scatter | solution.py:39
  656.8 0.0 copy-start
  656.8 4.2 copy.12
  661.0 2.6 bitcast_multiply_fusion
  663.6 284.2 %all-reduce.2.cloned.1.call-done = f32[8,256,2048]{2,1,0:T(8,128)} async-done(((f32[8,256,2048]{2,1,0:T(8,128)}), f32[8,256,2048]{2,1,0:T(8,128)}) %all-reduce.2.cloned.1.call-update) | async-done | bytes 16777232 | tf_op jit(solution)/shard_map/psum | solution.py:11
  947.8 31.9 %fusion.5 = f32[1024,512]{1,0:T(8,128)} fusion(f32[512,8,256]{2,1,0:T(8,128)} %bitcast_multiply_fusion, f32[8,256,2048]{2,1,0:T(8,128)} %all-reduce.2.cloned.1.call-done, s32[]{:T(128)S(6)} %select_n.50, f32[8]{0:T(128)S(1)} %dynamic-slice_reduce_fusion.2), kind=kOutput, calls=%fused_computation.9 | convolution fusion | flops 12886999040 | bytes 14680100 | tf_op jit(solution)/shard_map/iu,vi->uv/dot_general | solution.py:56
  979.6 0.0 reduce-scatter.5.cloned.1.call-update
  979.7 44.0 %reduce-scatter.5.cloned.1.call-done = f32[256,512]{1,0:T(8,128)} async-done(((f32[1024,512]{1,0:T(8,128)}), f32[256,512]{1,0:T(8,128)}) %reduce-scatter.5.cloned.1.call-update) | async-done | bytes 524304 | tf_op jit(solution)/shard_map/reduce_scatter | solution.py:59
  1023.7 0.0 copy-done
  1023.7 1.9 sub.9
  (1 shorter events, 0.0 us)
Async XLA Ops:
  7.2 291.9 %all-gather.2.cloned.1.call-start = ((), (), s32[]{:S(2)}) async-start(), calls=%async_computation.2 | async-start | bytes 20971520 | tf_op jit(solution)/shard_map/all_gather | solution.py:33
  7.9 648.9 %reduce-scatter.3.cloned.1.call-start = ((), (), s32[]{:S(2)}) async-start(), calls=%async_computation.3 | async-start | bytes 20971520 | tf_op jit(solution)/shard_map/reduce_scatter | solution.py:39
  532.3 415.5 %all-reduce.2.cloned.1.call-start = ((), (), s32[]{:S(2)}) async-start(), calls=%async_computation.4 | async-start | bytes 33554432 | tf_op jit(solution)/shard_map/psum | solution.py:11
  533.0 490.6 %reduce-scatter.5.cloned.1.call-start = ((), (), s32[]{:S(2)}) async-start(), calls=%async_computation.5 | async-start | bytes 2621440 | tf_op jit(solution)/shard_map/reduce_scatter | solution.py:59
  656.8 366.9 %copy-start = (f32[256,512]{1,0:T(8,128)S(1)}, f32[256,512]{1,0:T(8,128)}, u32[]{:S(2)}) copy-start(f32[256,512]{1,0:T(8,128)} %param.7) | copy-start | bytes 1572868
Sparse Core Ops, SparseCore 0:
  9.6 289.4 all-gather.1
  532.4 124.2 reduce-scatter.2
  659.4 288.2 all-reduce.1
  979.8 43.8 reduce-scatter.4
where the time goes:
time: 1030 us
  waiting for transfers between devices  727 us (71%)
  matrix products  248 us (24%)
  other arithmetic  22.5 us (2%)
  local copies, waits for them, and re-layouts  20.7 us (2%)
  between operations  13.8 us (1%)
    psum x1, waiting for transfers between devices, broadcast(): return lax.psum(block, axis)  284 us
    all_gather x1, waiting for transfers between devices, local(): panel = lax.all_gather(factor_panel, 'row', axis=2, tiled=True)  274 us
    dot_general x1, matrix products, local(): jnp.dot(matrix, masked_panel, precision=precise)  216 us
    reduce_scatter x1, waiting for transfers between devices, local(): lax.psum_scatter(-jnp.dot(matrix, masked_panel, precision=precise).T, 'co...  123 us
    reduce_scatter x1, waiting for transfers between devices, local(): lax.psum_scatter(partial_block, 'row', scatter_dimension=0, tiled=True)  44 us
    dot_general x1, matrix products, local(): jnp.einsum('iu,vi->uv', left_rows, upper.reshape(slice_width, rows_here),...  31.9 us
  transfers between devices with their start and end apart: 4, of which 4 were waited for; matrix products, arithmetic and copies ran while one was open for 2% of the time, Pallas kernels for 0%

commit v1 on v0

v1 whole, which is shorter than its diff:
```python
import functools

import jax
import jax.numpy as jnp
from jax import lax
from jax.experimental import pallas as pl
from jax.experimental.pallas import tpu as pltpu
from jax.sharding import PartitionSpec as P

CHUNK = 128


def halves(x):
    high = lax.reduce_precision(x, 8, 7)
    return high.astype(jnp.bfloat16), (x - high).astype(jnp.bfloat16)


def product_kernel(blocks, groups, mask_ref, panel_ref, high_ref, low_ref, out_ref, left_high, left_low):
    depth, chunk = panel_ref.shape[1:]
    width = depth // groups

    @pl.when(pl.program_id(0) == 0)
    def _():
        for b in range(blocks):
            for t in range(groups):
                span = slice(t * width, (t + 1) * width)
                x = (panel_ref[b, span, :] * mask_ref[b, t]).T
                high = x.astype(jnp.bfloat16)
                left_high[b * chunk : (b + 1) * chunk, span] = high
                low = x - high.astype(jnp.float32)
                left_low[b * chunk : (b + 1) * chunk, span] = low.astype(jnp.bfloat16)

    def dot(a, b):
        return lax.dot_general(a[...], b[...], (((1,), (1,)), ((), ())), preferred_element_type=jnp.float32)

    out_ref[...] = dot(left_high, high_ref) + (dot(left_high, low_ref) + dot(left_low, high_ref))


def block_product(mask, panel, high, low, first, order):
    blocks, depth, chunk = panel.shape
    tile = min(256, order)
    start = first // tile
    return pl.pallas_call(
        functools.partial(product_kernel, blocks, mask.shape[1]),
        grid=(order // tile,),
        out_shape=jax.ShapeDtypeStruct((blocks * chunk, order), jnp.float32),
        in_specs=[
            pl.BlockSpec(memory_space=pltpu.SMEM),
            pl.BlockSpec((blocks, depth, chunk), lambda i: (0, 0, 0)),
            pl.BlockSpec((tile, depth), lambda i: (start + i, 0)),
            pl.BlockSpec((tile, depth), lambda i: (start + i, 0)),
        ],
        out_specs=pl.BlockSpec((blocks * chunk, tile), lambda i: (0, i)),
        scratch_shapes=[pltpu.VMEM((blocks * chunk, depth), jnp.bfloat16)] * 2,
        compiler_params=pltpu.CompilerParams(vmem_limit_bytes=40 * 2**20),
        cost_estimate=pl.CostEstimate(
            flops=6 * blocks * chunk * depth * order,
            bytes_accessed=4 * (depth * order + blocks * chunk * (depth + order)),
            transcendentals=0,
        ),
    )(mask, panel, high, low)


def reduce_cols(partial):
    cols = lax.axis_size("col")
    col = lax.axis_index("col")
    pair = 2 if cols % 2 == 0 else 1
    far = cols // pair
    here, core = col // pair, col % pair
    part = partial.reshape((far, pair) + partial.shape[1:])
    if pair == 2:
        mine = lax.dynamic_index_in_dim(part, core, 1, False)
        other = lax.dynamic_index_in_dim(part, 1 - core, 1, False)
        swap = [(c, c ^ 1) for c in range(cols)]
        part = mine + lax.ppermute(other, "col", swap)
    else:
        part = part[:, 0]
    total = lax.dynamic_index_in_dim(part, here, 0, False)
    for step in range(1, far):
        send = lax.dynamic_index_in_dim(part, (here + step) % far, 0, False)
        pairs = [(c, ((c // pair + step) % far) * pair + c % pair) for c in range(cols)]
        total = total + lax.ppermute(send, "col", pairs)
    return total


def own_rows_of(panel, rows, cols, group):
    row, col = lax.axis_index("row"), lax.axis_index("col")
    slices = panel.reshape((cols, rows // cols) + panel.shape[1:])
    holder = row % cols
    kept = lax.dynamic_index_in_dim(slices, col, 0, False)
    kept = jnp.where(holder == col, kept, jnp.zeros_like(kept))
    for step in range(1, cols):
        send = lax.dynamic_index_in_dim(slices, (col + step) % cols, 0, False)
        pairs = [(r * cols + r % cols, r * cols + (r % cols + step) % cols) for r in range(rows)]
        kept = kept + lax.ppermute(send, ("row", "col"), pairs)
    found = [kept]
    for step in range(1, group):
        pairs = [(c, c // group * group + (c % group + step) % group) for c in range(cols)]
        found.append(lax.ppermute(kept, "col", pairs))
    found = jnp.stack(found)
    place = col % group
    return [lax.dynamic_index_in_dim(found, (place - p) % group, 0, False) for p in range(group)]


def local(root_inverse, factor_panel, struct_mask, child_diag_inverse):
    rows, cols = lax.axis_size("row"), lax.axis_size("col")
    row, col = lax.axis_index("row"), lax.axis_index("col")
    local_rows, width, local_cols, _ = root_inverse.shape
    rows_here, cols_here = local_rows * width, local_cols * width
    block = factor_panel.shape[2]
    total = block * rows
    children = struct_mask.shape[0]
    child_width = total // children
    slice_width = total // cols
    chunk = min(CHUNK, block)
    ratio = rows // cols
    mask = struct_mask.astype(jnp.float32)
    mask_cols = lax.dynamic_index_in_dim(mask.reshape(children, local_cols, cols), col, 2, False)
    mask_rows = lax.dynamic_index_in_dim(mask.reshape(children, local_rows, rows), row, 2, False)
    spread = jnp.repeat(mask_cols, rows // children, axis=0)
    child_here = col * slice_width // child_width
    own_mask = jnp.repeat(lax.dynamic_index_in_dim(mask_rows, child_here, 0, False), width)

    high, low = halves(root_inverse.reshape(rows_here, cols_here))
    uppers, lefts = [], []
    pieces_here = [factor_panel[:, :, first : first + chunk] for first in range(0, block, chunk)]
    pieces_here = list(lax.optimization_barrier(tuple(pieces_here)))
    following = lax.all_gather(pieces_here[0], "row", axis=0)
    following, high, low = lax.optimization_barrier((following, high, low))
    for step in range(len(pieces_here)):
        panel = following
        if step + 1 < len(pieces_here):
            panel, after = lax.optimization_barrier((panel, pieces_here[step + 1]))
            following = lax.all_gather(after, "row", axis=0)
        panel = panel.reshape(rows, cols_here, chunk)
        own = lax.dynamic_index_in_dim(
            panel.reshape(rows, local_rows, ratio, width, chunk), row // cols, 2, False
        )
        own = own_rows_of(own.reshape(rows, rows_here, chunk), rows, cols, cols // children)
        last = step + 1 == len(pieces_here)
        pieces = 2 if last and rows_here % 512 == 0 else 1
        height = rows_here // pieces
        found = []
        for first in range(0, rows_here, height):
            product = block_product(spread, panel, high, low, first, height)
            found.append(reduce_cols(product.reshape(cols, ratio, chunk, height)))
        uppers.append(-jnp.concatenate(found, axis=2) * own_mask)
        lefts.append(own)
        if not last:
            following, uppers[-1], lefts[-1] = lax.optimization_barrier((following, uppers[-1], lefts[-1]))
    upper = jnp.concatenate(uppers, axis=1).reshape(slice_width, rows_here)
    left = jnp.stack([jnp.concatenate(part, axis=0) for part in lefts], axis=1)
    left_mask = lax.dynamic_index_in_dim(mask_rows, child_here, 0, True)
    left_mask = jnp.repeat(left_mask, left.shape[0] * left.shape[1], axis=0)
    left = left.reshape(-1, rows_here, chunk)
    partial = block_product(left_mask, left, *halves(upper), 0, slice_width)
    reduced = lax.psum_scatter(partial, "row", scatter_dimension=0, tiled=True)
    return (upper.reshape(slice_width, local_rows, width), child_diag_inverse - reduced)


def solution(mesh):
    return jax.shard_map(
        local,
        mesh=mesh,
        in_specs=(
            P("poles", "row", None, "col"),
            P("poles", "col", "row"),
            P(),
            P("row", ("poles", "col")),
        ),
        out_specs=(P(("poles", "col"), None, "row"), P("row", ("poles", "col"))),
        check_vma=False,
    )
```

time: 1030 us -> 492 us (0.48)
  waiting for transfers between devices: 727 us -> 284 us
  matrix products: 248 us -> 0 us
  Pallas kernels: 0 us -> 86.9 us
  starting transfers between devices: 0.16 us -> 37 us
  local copies, waits for them, and re-layouts: 20.7 us -> 36.7 us
    psum x1 -> x0, waiting for transfers between devices: 284 us -> none  [broadcast(): return lax.psum(block, axis)]
    dot_general x2 -> x0, matrix products: 248 us -> none  [the longest x1 216 us: local(): jnp.dot(matrix, masked_panel, precision=precise)]
    all_gather x1 -> x4, waiting for transfers between devices: 274 us -> 75.6 us  [the longest x1 65.5 us: local(): following = lax.all_gather(pieces_here[0], 'row', axis=0)]
    ppermute x0 -> x26, waiting for transfers between devices: none -> 169 us  [the longest x12 93.2 us: own_rows_of(): kept = kept + lax.ppermute(send, ('row', 'col'), pairs)]
    reduce_scatter x2 -> x1, waiting for transfers between devices: 167 us -> 38.8 us  [local(): reduced = lax.psum_scatter(partial, 'row', scatter_dimension=0, tiled=True)]
    pallas_call x0 -> x6, Pallas kernels: none -> 86.9 us  [block_product(): pl.pallas_call(functools.partial(product_kernel, blocks, mask.shape[1]),...]
    ppermute x0 -> x26, starting transfers between devices: none -> 36.8 us  [the longest x12 26.4 us: own_rows_of(): kept = kept + lax.ppermute(send, ('row', 'col'), pairs)]
    select_n x1 -> x0, other arithmetic: 17.2 us -> none  [broadcast(): jnp.where(lax.axis_index(axis) == holder, block, jnp.zeros_like(block))]
  transfers between devices with their start and end apart: 4 -> 31, of which waited for: 4 -> 17; matrix products, arithmetic and copies ran while one was open for 2% -> 9% of each run, Pallas kernels for 0% -> 11%
where the time goes in v1:
time: 492 us; the launch traced here: 491 us
  waiting for transfers between devices  284 us (58%)
  Pallas kernels  86.9 us (18%)
  starting transfers between devices  37 us (8%)
  local copies, waits for them, and re-layouts  36.7 us (7%)
  other arithmetic  32 us (7%)
  between operations  14.4 us (3%)
    ppermute x12, waiting for transfers between devices, own_rows_of(): kept = kept + lax.ppermute(send, ('row', 'col'), pairs)  93.2 us
    pallas_call x6, Pallas kernels, block_product(): pl.pallas_call(functools.partial(product_kernel, blocks, mask.shape[1]),...  86.9 us
    ppermute x5, waiting for transfers between devices, reduce_cols(): total = total + lax.ppermute(send, 'col', pairs)  76.1 us
    all_gather x1, waiting for transfers between devices, local(): following = lax.all_gather(pieces_here[0], 'row', axis=0)  65.5 us
    reduce_scatter x1, waiting for transfers between devices, local(): reduced = lax.psum_scatter(partial, 'row', scatter_dimension=0, tiled=True)  38.8 us
    ppermute x12, starting transfers between devices, own_rows_of(): kept = kept + lax.ppermute(send, ('row', 'col'), pairs)  26.4 us
    unnamed x37, local copies, waits for them, and re-layouts  25.8 us
    all_gather x3, waiting for transfers between devices, local(): following = lax.all_gather(after, 'row', axis=0)  10.1 us
  transfers between devices with their start and end apart: 31, of which 17 were waited for; matrix products, arithmetic and copies ran while one was open for 9% of the time, Pallas kernels for 11%

profile of v1, /device:TPU:0, one launch (start us, length us, event | category | flops | bytes accessed | tf_op | source)
XLA Modules:
  0.0 490.8 jit_solution(17325743706315364660)
XLA Ops:
  7.2 4.4 fusion.34
  11.7 11.0 %copy.18 = f32[256,8,8,256]{3,1,2,0:T(8,128)S(1)} copy(f32[256,8,8,256]{3,2,1,0:T(8,128)} %bitcast.213) | data formatting | bytes 33554432
  22.7 7.0 %fusion = (bf16[2048,2048]{1,0:T(8,128)(2,1)}, bf16[2048,2048]{1,0:T(8,128)(2,1)}) fusion(f32[2048,2048]{1,0:T(8,128)S(1)} %bitcast.212), kind=kLoop, calls=%fused_computation.2 | loop fusion | flops 16777216 | bytes 33554432 | tf_op jit(solution)/shard_map/convert_element_type | solution.py:15
  29.7 65.5 %all-gather.9.cloned.1.call-done = f32[32,256,128]{2,1,0:T(8,128)} async-done(((f32[8,256,128]{2,1,0:T(8,128)}), f32[32,256,128]{2,1,0:T(8,128)}) %all-gather.9.cloned.1.call-update) | async-done | bytes 4194320 | tf_op jit(solution)/shard_map/all_gather | solution.py:128
  95.6 2.2 copy-done.3
  97.8 17.6 %shard_map.59 = f32[512,2048]{1,0:T(8,128)S(1)} custom-call(f32[4,8]{1,0:T(4,128)S(1)} %bitcast.207, f32[4,2048,128]{2,1,0:T(8,128)S(1)} %bitcast.195, bf16[2048,2048]{1,0:T(8,128)(2,1)} %get-tuple-element.32.high_ref, bf16[2048,2048]{1,0:T(8,128)(2,1)} %get-tuple-element.33.low_ref), custom_call_target="tpu_custom_call" | custom-call | flops 12884901888 | bytes 25165824 | tf_op jit(solution)/shard_map/pallas_call | solution.py:43
  115.6 1.9 copy-done
  117.5 3.4 dynamic-slice_bitcast_fusion.18
  120.8 3.4 collective-permute-start.2
  124.2 2.7 collective-permute-start.3
  126.9 2.3 collective-permute-start.4
  129.2 9.3 %collective-permute-done.3 = f32[1,2048,128]{2,1,0:T(8,128)} collective-permute-done((f32[1,2048,128]{2,1,0:T(8,128)}, f32[1,2048,128]{2,1,0:T(8,128)}, u32[]{:S(2)}, u32[]{:S(2)}) %collective-permute-start.3) | collective-permute-done | bytes 1048608 | tf_op jit(solution)/shard_map/ppermute | solution.py:95
  138.5 11.1 %collective-permute-done.4 = f32[1,2048,128]{2,1,0:T(8,128)} collective-permute-done((f32[1,2048,128]{2,1,0:T(8,128)S(1)}, f32[1,2048,128]{2,1,0:T(8,128)}, u32[]{:S(2)}, u32[]{:S(2)}) %collective-permute-start.4) | collective-permute-done | bytes 1048608 | tf_op jit(solution)/shard_map/ppermute | solution.py:95
  149.6 2.5 fusion.29
  153.1 1.8 bitcast_add_fusion.2
  158.1 2.8 fusion.15
  160.9 21.4 %collective-permute-done.1 = f32[1,128,2048]{2,1,0:T(8,128)} collective-permute-done((f32[1,128,2048]{2,1,0:T(8,128)}, f32[1,128,2048]{2,1,0:T(8,128)}, u32[]{:S(2)}, u32[]{:S(2)}) %collective-permute-start.1) | collective-permute-done | bytes 1048608 | tf_op jit(solution)/shard_map/ppermute | solution.py:82
  183.9 2.2 copy-done.2
  186.0 17.6 %shard_map.60 = f32[512,2048]{1,0:T(8,128)S(1)} custom-call(f32[4,8]{1,0:T(4,128)S(1)} %bitcast.208, f32[4,2048,128]{2,1,0:T(8,128)S(1)} %bitcast.190, bf16[2048,2048]{1,0:T(8,128)(2,1)} %get-tuple-element.32.high_ref, bf16[2048,2048]{1,0:T(8,128)(2,1)} %get-tuple-element.33.low_ref), custom_call_target="tpu_custom_call" | custom-call | flops 12884901888 | bytes 25165824 | tf_op jit(solution)/shard_map/pallas_call | solution.py:43
  204.3 3.7 collective-permute-start.10
  210.9 9.3 %collective-permute-done.10 = f32[1,2048,128]{2,1,0:T(8,128)S(1)} collective-permute-done((f32[1,2048,128]{2,1,0:T(8,128)S(1)}, f32[1,2048,128]{2,1,0:T(8,128)S(1)}, u32[]{:S(2)}, u32[]{:S(2)}) %collective-permute-start.10) | collective-permute-done | bytes 1048608 | tf_op jit(solution)/shard_map/ppermute | solution.py:95
  220.3 11.2 %collective-permute-done.9 = f32[1,2048,128]{2,1,0:T(8,128)S(1)} collective-permute-done((f32[1,2048,128]{2,1,0:T(8,128)S(1)}, f32[1,2048,128]{2,1,0:T(8,128)S(1)}, u32[]{:S(2)}, u32[]{:S(2)}) %collective-permute-start.9) | collective-permute-done | bytes 1048608 | tf_op jit(solution)/shard_map/ppermute | solution.py:95
  232.2 2.5 collective-permute-start.7
  236.4 22.2 %collective-permute-done.7 = f32[1,128,2048]{2,1,0:T(8,128)S(1)} collective-permute-done((f32[1,128,2048]{2,1,0:T(8,128)S(1)}, f32[1,128,2048]{2,1,0:T(8,128)S(1)}, u32[]{:S(2)}, u32[]{:S(2)}) %collective-permute-start.7) | collective-permute-done | bytes 1048608 | tf_op jit(solution)/shard_map/ppermute | solution.py:82
  258.7 4.4 all-gather.13.cloned.1.call-done
  263.2 2.2 copy-done.5
  265.4 17.7 %shard_map.61 = f32[512,2048]{1,0:T(8,128)S(1)} custom-call(f32[4,8]{1,0:T(4,128)S(1)} %bitcast.209, f32[4,2048,128]{2,1,0:T(8,128)S(1)} %bitcast.200, bf16[2048,2048]{1,0:T(8,128)(2,1)} %get-tuple-element.32.high_ref, bf16[2048,2048]{1,0:T(8,128)(2,1)} %get-tuple-element.33.low_ref), custom_call_target="tpu_custom_call" | custom-call | flops 12884901888 | bytes 25165824 | tf_op jit(solution)/shard_map/pallas_call | solution.py:43
  283.6 2.5 collective-permute-start.14
  289.2 10.9 %collective-permute-done.15 = f32[1,2048,128]{2,1,0:T(8,128)S(1)} collective-permute-done((f32[1,2048,128]{2,1,0:T(8,128)S(1)}, f32[1,2048,128]{2,1,0:T(8,128)S(1)}, u32[]{:S(2)}, u32[]{:S(2)}) %collective-permute-start.15) | collective-permute-done | bytes 1048608 | tf_op jit(solution)/shard_map/ppermute | solution.py:95
  300.1 11.2 %collective-permute-done.16 = f32[1,2048,128]{2,1,0:T(8,128)S(1)} collective-permute-done((f32[1,2048,128]{2,1,0:T(8,128)S(1)}, f32[1,2048,128]{2,1,0:T(8,128)S(1)}, u32[]{:S(2)}, u32[]{:S(2)}) %collective-permute-start.16) | collective-permute-done | bytes 1048608 | tf_op jit(solution)/shard_map/ppermute | solution.py:95
  312.0 2.7 collective-permute-start.13
  316.5 21.7 %collective-permute-done.13 = f32[1,128,2048]{2,1,0:T(8,128)S(1)} collective-permute-done((f32[1,128,2048]{2,1,0:T(8,128)S(1)}, f32[1,128,2048]{2,1,0:T(8,128)S(1)}, u32[]{:S(2)}, u32[]{:S(2)}) %collective-permute-start.13) | collective-permute-done | bytes 1048608 | tf_op jit(solution)/shard_map/ppermute | solution.py:82
  338.3 5.6 %all-gather.15.cloned.1.call-done = f32[32,256,128]{2,1,0:T(8,128)} async-done(((f32[8,256,128]{2,1,0:T(8,128)}), f32[32,256,128]{2,1,0:T(8,128)}) %all-gather.15.cloned.1.call-update) | async-done | bytes 4194320 | tf_op jit(solution)/shard_map/all_gather | solution.py:134
  343.9 2.2 copy-done.4
  346.1 10.2 %shard_map.62 = f32[512,1024]{1,0:T(8,128)S(1)} custom-call(f32[4,8]{1,0:T(4,128)S(1)} %bitcast.210, f32[4,2048,128]{2,1,0:T(8,128)S(1)} %bitcast.196, bf16[2048,2048]{1,0:T(8,128)(2,1)} %get-tuple-element.32.high_ref, bf16[2048,2048]{1,0:T(8,128)(2,1)} %get-tuple-element.33.low_ref), custom_call_target="tpu_custom_call" | custom-call | flops 6442450944 | bytes 14680064 | tf_op jit(solution)/shard_map/pallas_call | solution.py:43
  356.3 10.2 %shard_map.63 = f32[512,1024]{1,0:T(8,128)S(1)} custom-call(f32[4,8]{1,0:T(4,128)S(1)} %bitcast.211, f32[4,2048,128]{2,1,0:T(8,128)S(1)} %bitcast.197, bf16[2048,2048]{1,0:T(8,128)(2,1)} %get-tuple-element.32.high_ref, bf16[2048,2048]{1,0:T(8,128)(2,1)} %get-tuple-element.33.low_ref), custom_call_target="tpu_custom_call" | custom-call | flops 6442450944 | bytes 14680064 | tf_op jit(solution)/shard_map/pallas_call | solution.py:43
  369.2 2.2 collective-permute-start.22
  371.4 2.4 collective-permute-start.23
  375.8 2.1 collective-permute-start.21
  377.9 18.8 %collective-permute-done.23 = f32[1,2048,128]{2,1,0:T(8,128)S(1)} collective-permute-done((f32[1,2048,128]{2,1,0:T(8,128)S(1)}, f32[1,2048,128]{2,1,0:T(8,128)S(1)}, u32[]{:S(2)}, u32[]{:S(2)}) %collective-permute-start.23) | collective-permute-done | bytes 1048608 | tf_op jit(solution)/shard_map/ppermute | solution.py:95
  396.7 11.2 %collective-permute-done.24 = f32[1,2048,128]{2,1,0:T(8,128)S(1)} collective-permute-done((f32[1,2048,128]{2,1,0:T(8,128)S(1)}, f32[1,2048,128]{2,1,0:T(8,128)S(1)}, u32[]{:S(2)}, u32[]{:S(2)}) %collective-permute-start.24) | collective-permute-done | bytes 1048608 | tf_op jit(solution)/shard_map/ppermute | solution.py:95
  408.3 5.2 %collective-permute-done.19 = f32[1,128,1024]{2,1,0:T(8,128)S(1)} collective-permute-done((f32[1,128,1024]{2,1,0:T(8,128)S(1)}, f32[1,128,1024]{2,1,0:T(8,128)S(1)}, u32[]{:S(2)}, u32[]{:S(2)}) %collective-permute-start.19) | collective-permute-done | bytes 524320 | tf_op jit(solution)/shard_map/ppermute | solution.py:82
  413.6 5.5 %collective-permute-done.21 = f32[1,128,1024]{2,1,0:T(8,128)S(1)} collective-permute-done((f32[1,128,1024]{2,1,0:T(8,128)S(1)}, f32[1,128,1024]{2,1,0:T(8,128)S(1)}, u32[]{:S(2)}, u32[]{:S(2)}) %collective-permute-start.21) | collective-permute-done | bytes 524320 | tf_op jit(solution)/shard_map/ppermute | solution.py:82
  421.9 3.6 pad_maximum_fusion
  425.5 13.6 %shard_map.64 = f32[1024,512]{1,0:T(8,128)} custom-call(f32[8,8]{1,0:T(8,128)S(1)} %reshape.187.mask_ref, f32[8,2048,128]{2,1,0:T(8,128)} %bitcast.217, bf16[512,2048]{1,0:T(8,128)(2,1)S(1)} %get-tuple-element.55.high_ref, bf16[512,2048]{1,0:T(8,128)(2,1)S(1)} %get-tuple-element.54.low_ref), custom_call_target="tpu_custom_call" | custom-call | flops 6442450944 | bytes 14680064 | tf_op jit(solution)/shard_map/pallas_call | solution.py:43
  441.2 2.3 pad_maximum_fusion.1
  443.5 38.8 %reduce-scatter.2.cloned.1.call-done = f32[256,512]{1,0:T(8,128)} async-done(((f32[1024,512]{1,0:T(8,128)}), f32[256,512]{1,0:T(8,128)}) %reduce-scatter.2.cloned.1.call-update) | async-done | bytes 524304 | tf_op jit(solution)/shard_map/reduce_scatter | solution.py:157
  482.3 1.9 sub.43
  (111 shorter events, 28.0 us)
Async XLA Ops:
  7.2 88.1 %all-gather.9.cloned.1.call-start = ((), (), s32[]{:S(2)}) async-start(), calls=%async_computation.2 | async-start | bytes 5242880 | tf_op jit(solution)/shard_map/all_gather | solution.py:128
  11.6 172.2 %all-gather.11.cloned.1.call-start = ((), (), s32[]{:S(2)}) async-start(), calls=%async_computation.3 | async-start | bytes 5242880 | tf_op jit(solution)/shard_map/all_gather | solution.py:134
  22.7 72.6 %copy-start.14 = (s32[2,32]{1,0:T(2,128)S(1)}, s32[2,32]{1,0:T(2,128)}, u32[]{:S(2)}) copy-start(s32[2,32]{1,0:T(2,128)} %param.6) | copy-start | bytes 772
  95.3 167.9 %all-gather.13.cloned.1.call-start = ((), (), s32[]{:S(2)}) async-start(), calls=%async_computation.4 | async-start | bytes 5242880 | tf_op jit(solution)/shard_map/all_gather | solution.py:134
  95.6 2.2 copy-start.3
  115.4 2.0 copy-start
  117.5 34.8 %collective-permute-start = (f32[2,1,128,2048]{3,2,1,0:T(8,128)S(1)}, f32[2,1,128,2048]{3,2,1,0:T(8,128)}, u32[]{:S(2)}, u32[]{:S(2)}) collective-permute-start(f32[2,1,128,2048]{3,2,1,0:T(8,128)S(1)} %dynamic-slice_bitcast_fusion.2), channel_id=1, source_target_pairs={{0,1},{1,0},{2,3},{3,2},{4,5},{5,4},{6,7},{7,6},{8,9},{9,8},{10,11... | collective-permute-start | bytes 6291464 | tf_op jit(solution)/shard_map/ppermute | solution.py:75
  120.8 8.3 %collective-permute-start.2 = (f32[1,2048,128]{2,1,0:T(8,128)}, f32[1,2048,128]{2,1,0:T(8,128)}, u32[]{:S(2)}, u32[]{:S(2)}) collective-permute-start(f32[1,2048,128]{2,1,0:T(8,128)} %get-tuple-element.65), channel_id=1, source_target_pairs={{0,1},{5,6},{10,11},{15,12},{16,17},{21,22},{26,27},{31,28}} | collective-permute-start | bytes 3145736 | tf_op jit(solution)/shard_map/ppermute | solution.py:95
  124.2 14.3 %collective-permute-start.3 = (f32[1,2048,128]{2,1,0:T(8,128)}, f32[1,2048,128]{2,1,0:T(8,128)}, u32[]{:S(2)}, u32[]{:S(2)}) collective-permute-start(f32[1,2048,128]{2,1,0:T(8,128)} %get-tuple-element.66), channel_id=1, source_target_pairs={{0,2},{5,7},{10,8},{15,13},{16,18},{21,23},{26,24},{31,29}} | collective-permute-start | bytes 3145736 | tf_op jit(solution)/shard_map/ppermute | solution.py:95
  126.9 22.7 %collective-permute-start.4 = (f32[1,2048,128]{2,1,0:T(8,128)S(1)}, f32[1,2048,128]{2,1,0:T(8,128)}, u32[]{:S(2)}, u32[]{:S(2)}) collective-permute-start(f32[1,2048,128]{2,1,0:T(8,128)S(1)} %get-tuple-element.67), channel_id=1, source_target_pairs={{0,3},{5,4},{10,9},{15,14},{16,19},{21,20},{26,25},{31,30}} | collective-permute-start | bytes 3145736 | tf_op jit(solution)/shard_map/ppermute | solution.py:95
  149.6 3.5 copy-start.1
  152.2 5.9 %collective-permute-start.5 = (f32[1,2048,128]{2,1,0:T(8,128)S(1)}, f32[1,2048,128]{2,1,0:T(8,128)}, u32[]{:S(2)}, u32[]{:S(2)}) collective-permute-start(f32[1,2048,128]{2,1,0:T(8,128)S(1)} %fusion.29), channel_id=1, source_target_pairs={{0,1},{1,0},{2,3},{3,2},{4,5},{5,4},{6,7},{7,6},{8,9},{9,8},{10,11... | collective-permute-start | bytes 3145736 | tf_op jit(solution)/shard_map/ppermute | solution.py:99
  156.0 26.3 %collective-permute-start.1 = (f32[1,128,2048]{2,1,0:T(8,128)}, f32[1,128,2048]{2,1,0:T(8,128)}, u32[]{:S(2)}, u32[]{:S(2)}) collective-permute-start(f32[1,128,2048]{2,1,0:T(8,128)} %dynamic-slice_bitcast_fusion.19), channel_id=1, source_target_pairs={{0,2},{1,3},{2,0},{3,1},{4,6},{5,7},{6,4},{7,5},{8,10},{9,11},{10,... | collective-permute-start | bytes 3145736 | tf_op jit(solution)/shard_map/ppermute | solution.py:82
  183.8 160.1 %all-gather.15.cloned.1.call-start = ((), (), s32[]{:S(2)}) async-start(), calls=%async_computation.5 | async-start | bytes 5242880 | tf_op jit(solution)/shard_map/all_gather | solution.py:134
  183.9 2.2 copy-start.2
  203.9 27.8 %collective-permute-start.6 = (f32[2,1,128,2048]{3,2,1,0:T(8,128)S(1)}, f32[2,1,128,2048]{3,2,1,0:T(8,128)S(1)}, u32[]{:S(2)}, u32[]{:S(2)}) collective-permute-start(f32[2,1,128,2048]{3,2,1,0:T(8,128)S(1)} %dynamic-slice_bitcast_fusion.1), channel_id=1, source_target_pairs={{0,1},{1,0},{2,3},{3,2},{4,5},{5,4},{6,7},{7,6},{8,9},{9,8},{10,11... | collective-permute-start | bytes 6291464 | tf_op jit(solution)/shard_map/ppermute | solution.py:75
  204.3 16.0 %collective-permute-start.10 = (f32[1,2048,128]{2,1,0:T(8,128)S(1)}, f32[1,2048,128]{2,1,0:T(8,128)S(1)}, u32[]{:S(2)}, u32[]{:S(2)}) collective-permute-start(f32[1,2048,128]{2,1,0:T(8,128)S(1)} %get-tuple-element.64), channel_id=1, source_target_pairs={{0,3},{5,4},{10,9},{15,14},{16,19},{21,20},{26,25},{31,30}} | collective-permute-start | bytes 3145736 | tf_op jit(solution)/shard_map/ppermute | solution.py:95
  208.0 12.2 %collective-permute-start.8 = (f32[1,2048,128]{2,1,0:T(8,128)S(1)}, f32[1,2048,128]{2,1,0:T(8,128)S(1)}, u32[]{:S(2)}, u32[]{:S(2)}) collective-permute-start(f32[1,2048,128]{2,1,0:T(8,128)S(1)} %get-tuple-element.62), channel_id=1, source_target_pairs={{0,1},{5,6},{10,11},{15,12},{16,17},{21,22},{26,27},{31,28}} | collective-permute-start | bytes 3145736 | tf_op jit(solution)/shard_map/ppermute | solution.py:95
  209.4 22.1 %collective-permute-start.9 = (f32[1,2048,128]{2,1,0:T(8,128)S(1)}, f32[1,2048,128]{2,1,0:T(8,128)S(1)}, u32[]{:S(2)}, u32[]{:S(2)}) collective-permute-start(f32[1,2048,128]{2,1,0:T(8,128)S(1)} %get-tuple-element.63), channel_id=1, source_target_pairs={{0,2},{5,7},{10,8},{15,13},{16,18},{21,23},{26,24},{31,29}} | collective-permute-start | bytes 3145736 | tf_op jit(solution)/shard_map/ppermute | solution.py:95
  231.7 3.1 collective-permute-start.11
  232.2 26.4 %collective-permute-start.7 = (f32[1,128,2048]{2,1,0:T(8,128)S(1)}, f32[1,128,2048]{2,1,0:T(8,128)S(1)}, u32[]{:S(2)}, u32[]{:S(2)}) collective-permute-start(f32[1,128,2048]{2,1,0:T(8,128)S(1)} %dynamic-slice_bitcast_fusion.15), channel_id=1, source_target_pairs={{0,2},{1,3},{2,0},{3,1},{4,6},{5,7},{6,4},{7,5},{8,10},{9,11},{10,... | collective-permute-start | bytes 3145736 | tf_op jit(solution)/shard_map/ppermute | solution.py:82
  263.2 219.1 %reduce-scatter.2.cloned.1.call-start = ((), (), s32[]{:S(2)}) async-start(), calls=%async_computation.1 | async-start | bytes 2621440 | tf_op jit(solution)/shard_map/reduce_scatter | solution.py:157
  263.2 2.2 copy-start.5
  283.3 28.3 %collective-permute-start.12 = (f32[2,1,128,2048]{3,2,1,0:T(8,128)S(1)}, f32[2,1,128,2048]{3,2,1,0:T(8,128)S(1)}, u32[]{:S(2)}, u32[]{:S(2)}) collective-permute-start(f32[2,1,128,2048]{3,2,1,0:T(8,128)S(1)} %dynamic-slice_bitcast_fusion), channel_id=1, source_target_pairs={{0,1},{1,0},{2,3},{3,2},{4,5},{5,4},{6,7},{7,6},{8,9},{9,8},{10,11... | collective-permute-start | bytes 6291464 | tf_op jit(solution)/shard_map/ppermute | solution.py:75
  283.6 5.6 %collective-permute-start.14 = (f32[1,2048,128]{2,1,0:T(8,128)S(1)}, f32[1,2048,128]{2,1,0:T(8,128)S(1)}, u32[]{:S(2)}, u32[]{:S(2)}) collective-permute-start(f32[1,2048,128]{2,1,0:T(8,128)S(1)} %get-tuple-element.59), channel_id=1, source_target_pairs={{0,1},{5,6},{10,11},{15,12},{16,17},{21,22},{26,27},{31,28}} | collective-permute-start | bytes 3145736 | tf_op jit(solution)/shard_map/ppermute | solution.py:95
  286.1 14.0 %collective-permute-start.15 = (f32[1,2048,128]{2,1,0:T(8,128)S(1)}, f32[1,2048,128]{2,1,0:T(8,128)S(1)}, u32[]{:S(2)}, u32[]{:S(2)}) collective-permute-start(f32[1,2048,128]{2,1,0:T(8,128)S(1)} %get-tuple-element.60), channel_id=1, source_target_pairs={{0,2},{5,7},{10,8},{15,13},{16,18},{21,23},{26,24},{31,29}} | collective-permute-start | bytes 3145736 | tf_op jit(solution)/shard_map/ppermute | solution.py:95
  287.8 23.5 %collective-permute-start.16 = (f32[1,2048,128]{2,1,0:T(8,128)S(1)}, f32[1,2048,128]{2,1,0:T(8,128)S(1)}, u32[]{:S(2)}, u32[]{:S(2)}) collective-permute-start(f32[1,2048,128]{2,1,0:T(8,128)S(1)} %get-tuple-element.61), channel_id=1, source_target_pairs={{0,3},{5,4},{10,9},{15,14},{16,19},{21,20},{26,25},{31,30}} | collective-permute-start | bytes 3145736 | tf_op jit(solution)/shard_map/ppermute | solution.py:95
  311.5 3.3 collective-permute-start.17
  312.0 26.1 %collective-permute-start.13 = (f32[1,128,2048]{2,1,0:T(8,128)S(1)}, f32[1,128,2048]{2,1,0:T(8,128)S(1)}, u32[]{:S(2)}, u32[]{:S(2)}) collective-permute-start(f32[1,128,2048]{2,1,0:T(8,128)S(1)} %dynamic-slice_bitcast_fusion.11), channel_id=1, source_target_pairs={{0,2},{1,3},{2,0},{3,1},{4,6},{5,7},{6,4},{7,5},{8,10},{9,11},{10,... | collective-permute-start | bytes 3145736 | tf_op jit(solution)/shard_map/ppermute | solution.py:82
  343.9 2.2 copy-start.4
  366.5 1.2 copy-start.9
  366.5 1.5 copy-start.10
  366.5 1.8 copy-start.11
  366.5 2.1 copy-start.12
  366.6 8.7 %collective-permute-start.18 = (f32[2,1,128,1024]{3,2,1,0:T(8,128)S(1)}, f32[2,1,128,1024]{3,2,1,0:T(8,128)S(1)}, u32[]{:S(2)}, u32[]{:S(2)}) collective-permute-start(f32[2,1,128,1024]{3,2,1,0:T(8,128)S(1)} %dynamic-slice_bitcast_fusion.7), channel_id=1, source_target_pairs={{0,1},{1,0},{2,3},{3,2},{4,5},{5,4},{6,7},{7,6},{8,9},{9,8},{10,11... | collective-permute-start | bytes 3145736 | tf_op jit(solution)/shard_map/ppermute | solution.py:75
  366.8 8.8 %collective-permute-start.20 = (f32[2,1,128,1024]{3,2,1,0:T(8,128)S(1)}, f32[2,1,128,1024]{3,2,1,0:T(8,128)S(1)}, u32[]{:S(2)}, u32[]{:S(2)}) collective-permute-start(f32[2,1,128,1024]{3,2,1,0:T(8,128)S(1)} %dynamic-slice_bitcast_fusion.6), channel_id=1, source_target_pairs={{0,1},{1,0},{2,3},{3,2},{4,5},{5,4},{6,7},{7,6},{8,9},{9,8},{10,11... | collective-permute-start | bytes 3145736 | tf_op jit(solution)/shard_map/ppermute | solution.py:75
  369.0 6.2 %copy-start.7 = (f32[1,2048,128]{2,1,0:T(8,128)S(1)}, f32[1,2048,128]{2,1,0:T(8,128)}, u32[]{:S(2)}) copy-start(f32[1,2048,128]{2,1,0:T(8,128)} %get-tuple-element.51) | copy-start | bytes 3145732
  369.0 6.2 %copy-start.8 = (f32[1,2048,128]{2,1,0:T(8,128)S(1)}, f32[1,2048,128]{2,1,0:T(8,128)}, u32[]{:S(2)}) copy-start(f32[1,2048,128]{2,1,0:T(8,128)} %get-tuple-element.50) | copy-start | bytes 3145732
  369.2 8.7 %collective-permute-start.22 = (f32[1,2048,128]{2,1,0:T(8,128)S(1)}, f32[1,2048,128]{2,1,0:T(8,128)S(1)}, u32[]{:S(2)}, u32[]{:S(2)}) collective-permute-start(f32[1,2048,128]{2,1,0:T(8,128)S(1)} %get-tuple-element.56), channel_id=1, source_target_pairs={{0,1},{5,6},{10,11},{15,12},{16,17},{21,22},{26,27},{31,28}} | collective-permute-start | bytes 3145736 | tf_op jit(solution)/shard_map/ppermute | solution.py:95
  371.4 25.3 %collective-permute-start.23 = (f32[1,2048,128]{2,1,0:T(8,128)S(1)}, f32[1,2048,128]{2,1,0:T(8,128)S(1)}, u32[]{:S(2)}, u32[]{:S(2)}) collective-permute-start(f32[1,2048,128]{2,1,0:T(8,128)S(1)} %get-tuple-element.57), channel_id=1, source_target_pairs={{0,2},{5,7},{10,8},{15,13},{16,18},{21,23},{26,24},{31,29}} | collective-permute-start | bytes 3145736 | tf_op jit(solution)/shard_map/ppermute | solution.py:95
  373.8 34.1 %collective-permute-start.24 = (f32[1,2048,128]{2,1,0:T(8,128)S(1)}, f32[1,2048,128]{2,1,0:T(8,128)S(1)}, u32[]{:S(2)}, u32[]{:S(2)}) collective-permute-start(f32[1,2048,128]{2,1,0:T(8,128)S(1)} %get-tuple-element.58), channel_id=1, source_target_pairs={{0,3},{5,4},{10,9},{15,14},{16,19},{21,20},{26,25},{31,30}} | collective-permute-start | bytes 3145736 | tf_op jit(solution)/shard_map/ppermute | solution.py:95
  375.5 38.0 %collective-permute-start.19 = (f32[1,128,1024]{2,1,0:T(8,128)S(1)}, f32[1,128,1024]{2,1,0:T(8,128)S(1)}, u32[]{:S(2)}, u32[]{:S(2)}) collective-permute-start(f32[1,128,1024]{2,1,0:T(8,128)S(1)} %dynamic-slice_bitcast_fusion.21), channel_id=1, source_target_pairs={{0,2},{1,3},{2,0},{3,1},{4,6},{5,7},{6,4},{7,5},{8,10},{9,11},{10,... | collective-permute-start | bytes 1572872 | tf_op jit(solution)/shard_map/ppermute | solution.py:82
  375.8 43.3 %collective-permute-start.21 = (f32[1,128,1024]{2,1,0:T(8,128)S(1)}, f32[1,128,1024]{2,1,0:T(8,128)S(1)}, u32[]{:S(2)}, u32[]{:S(2)}) collective-permute-start(f32[1,128,1024]{2,1,0:T(8,128)S(1)} %dynamic-slice_bitcast_fusion.20), channel_id=1, source_target_pairs={{0,2},{1,3},{2,0},{3,1},{4,6},{5,7},{6,4},{7,5},{8,10},{9,11},{10,... | collective-permute-start | bytes 1572872 | tf_op jit(solution)/shard_map/ppermute | solution.py:82
  408.2 13.1 %collective-permute-start.25 = (f32[1,2048,128]{2,1,0:T(8,128)S(1)}, f32[1,2048,128]{2,1,0:T(8,128)S(1)}, u32[]{:S(2)}, u32[]{:S(2)}) collective-permute-start(f32[1,2048,128]{2,1,0:T(8,128)S(1)} %fusion.19), channel_id=1, source_target_pairs={{0,1},{1,0},{2,3},{3,2},{4,5},{5,4},{6,7},{7,6},{8,9},{9,8},{10,11... | collective-permute-start | bytes 3145736 | tf_op jit(solution)/shard_map/ppermute | solution.py:99
  439.5 1.2 copy-start.6
  441.2 41.1 %copy-start.13 = (f32[256,512]{1,0:T(8,128)S(1)}, f32[256,512]{1,0:T(8,128)}, u32[]{:S(2)}) copy-start(f32[256,512]{1,0:T(8,128)} %param.7) | copy-start | bytes 1572868
Sparse Core Ops, SparseCore 0:
  11.7 83.4 all-gather.8
  96.8 79.2 all-gather.10
  183.9 79.1 all-gather.12
  264.6 79.2 all-gather.14
  439.3 43.0 reduce-scatter.1
